TPU v7x, 32 devices: a whole 2x2x4 slice. The times are simulated.
32 devices in a mesh: row: 2 (over y), col: 16 (over z, x, core).
Axes of the slice: x: 2, y: 2, z: 4, core: 2. Of those that a mesh axis runs over, the one named last changes fastest.
Arguments:
- pixels: bfloat16 [6304, 768], P('row', 'col'), may hold values from -6 to 6
- mask_places: int32 [32, 80], P('col'), may hold values from 1 to 196, as said below
- mask_count: int32 [32], P('col'), may hold values from 40 to 80, as said below
- targets: int32 [32, 80], P('col'), may hold values from 0 to 8191
- step_count: int32 [1], replicated, may hold values from 1 to 20
- patch_weight: float32 [768, 768], P('col', 'row'), may hold values from -0.21875 to 0.21875
- vector_table: float32 [205, 768], P(None, 'row')
- input_weight: float32 [1, 768, 2304], P(None, 'row', 'col'), may hold values from -0.21875 to 0.21875
- output_weight: float32 [1, 768, 768], P(None, 'col', 'row'), may hold values from -0.625 to 0.625
- upward_weight: float32 [1, 768, 3072], P(None, 'row', 'col'), may hold values from -0.21875 to 0.21875
- downward_weight: float32 [1, 3072, 768], P(None, 'col', 'row'), may hold values from -0.109375 to 0.109375
- head_weight: float32 [768, 8192], P(None, 'row'), may hold values from -0.21875 to 0.21875
- drift_patch: float32 [768, 768], P('col', 'row'), may hold values from -4.5776367e-05 to 4.5776367e-05
- drift_table: float32 [205, 768], P(None, 'row'), may hold values from -4.5776367e-05 to 4.5776367e-05
- drift_input: float32 [1, 768, 2304], P(None, 'row', 'col'), may hold values from -4.5776367e-05 to 4.5776367e-05
- drift_output: float32 [1, 768, 768], P(None, 'col', 'row'), may hold values from -4.5776367e-05 to 4.5776367e-05
- drift_upward: float32 [1, 768, 3072], P(None, 'row', 'col'), may hold values from -4.5776367e-05 to 4.5776367e-05
- drift_downward: float32 [1, 3072, 768], P(None, 'col', 'row'), may hold values from -4.5776367e-05 to 4.5776367e-05
- drift_head: float32 [768, 8192], P(None, 'row'), may hold values from -4.5776367e-05 to 4.5776367e-05
- power_patch: float32 [768, 768], P('col', 'row'), may hold values from 2.1251565e-13 to 2.1251564e-12
- power_table: float32 [205, 768], P(None, 'row'), may hold values from 2.1251565e-13 to 2.1251564e-12
- power_input: float32 [1, 768, 2304], P(None, 'row', 'col'), may hold values from 2.1251565e-13 to 2.1251564e-12
- power_output: float32 [1, 768, 768], P(None, 'col', 'row'), may hold values from 2.1251565e-13 to 2.1251564e-12
- power_upward: float32 [1, 768, 3072], P(None, 'row', 'col'), may hold values from 2.1251565e-13 to 2.1251564e-12
- power_downward: float32 [1, 3072, 768], P(None, 'col', 'row'), may hold values from 2.1251565e-13 to 2.1251564e-12
- power_head: float32 [768, 8192], P(None, 'row'), may hold values from 2.1251565e-13 to 2.1251564e-12
Outputs:
- mean_loss: float32 [], replicated
- grad_norm: float32 [], replicated
- patch_update: float32 [768, 768], P('col', 'row')
- patch_drift: float32 [768, 768], P('col', 'row')
- patch_power: float32 [768, 768], P('col', 'row')
- table_update: float32 [205, 768], P(None, 'row')
- table_drift: float32 [205, 768], P(None, 'row')
- table_power: float32 [205, 768], P(None, 'row')
- input_update: float32 [1, 768, 2304], P(None, 'row', 'col')
- input_drift: float32 [1, 768, 2304], P(None, 'row', 'col')
- input_power: float32 [1, 768, 2304], P(None, 'row', 'col')
- output_update: float32 [1, 768, 768], P(None, 'col', 'row')
- output_drift: float32 [1, 768, 768], P(None, 'col', 'row')
- output_power: float32 [1, 768, 768], P(None, 'col', 'row')
- upward_update: float32 [1, 768, 3072], P(None, 'row', 'col')
- upward_drift: float32 [1, 768, 3072], P(None, 'row', 'col')
- upward_power: float32 [1, 768, 3072], P(None, 'row', 'col')
- downward_update: float32 [1, 3072, 768], P(None, 'col', 'row')
- downward_drift: float32 [1, 3072, 768], P(None, 'col', 'row')
- downward_power: float32 [1, 3072, 768], P(None, 'col', 'row')
- head_update: float32 [768, 8192], P(None, 'row')
- head_drift: float32 [768, 8192], P(None, 'row')
- head_power: float32 [768, 8192], P(None, 'row')
Inputs may be any that keep to these rules, and one draw needn't show every extreme that they name: `mask_places`: within each image the 80 places are distinct; slot j counts when j < mask_count of that image. `mask_count`: some image has exactly 80 counted slots.
All inputs are finite; a program needn't handle non-finite values.
Results may differ from a plain program's by a relative error of at most 0.024.
Values may be sent and summed in bfloat16 or wider, within the bound.
A program may use at most 256 MiB of HBM per device.

v0:
```python
import math
import jax
import jax.numpy as jnp
from jax import lax
from jax.sharding import PartitionSpec as P

HEADS = 12
HD = 64
SEQ = 197
MSLOT = 80
BOTH = ("row", "col")
norm_eps = 1e-06
clip_limit = 0.1
learn_rate = 0.01
beta_first = 0.9
beta_second = 0.999
adam_eps = 1e-08
weight_decay = 0.05
low_type = jnp.bfloat16
wide = jnp.float32


def product(left, right):
    return jnp.dot(left, right, preferred_element_type=wide)


def product_nt(left, right):
    return jnp.einsum("ab,cb->ac", left, right, preferred_element_type=wide)


def product_tn(left, right):
    return jnp.einsum("ab,ac->bc", left, right, preferred_element_type=wide)


def norm_forward(values, gain, shift):
    center = jnp.mean(values, axis=1, keepdims=True)
    moved = values - center
    inverse = lax.rsqrt(jnp.mean(moved * moved, axis=1, keepdims=True) + norm_eps)
    scaled = moved * inverse
    return (scaled * gain + shift, (scaled, inverse))


def norm_backward(upstream, kept, gain):
    scaled, inverse = kept
    inner = upstream * gain
    downstream = inverse * (
        inner
        - jnp.mean(inner, axis=1, keepdims=True)
        - scaled * jnp.mean(inner * scaled, axis=1, keepdims=True)
    )
    return (downstream, jnp.sum(upstream * scaled, axis=0), jnp.sum(upstream, axis=0))


def exact_gelu(values):
    return jax.nn.gelu(values, approximate=False)


def split_heads(grouped):
    images = grouped.shape[0] // SEQ
    pieces = grouped.reshape(images, SEQ, 3, HEADS, HD)
    return (pieces[:, :, 0], pieces[:, :, 1], pieces[:, :, 2])


def attention_weights(query, keys):
    scores = jnp.einsum("iqhd,ikhd->ihqk", query, keys, preferred_element_type=wide)
    return jax.nn.softmax(scores * (1.0 / math.sqrt(HD)), axis=-1)


def attend(grouped):
    query, keys, values = split_heads(grouped)
    weights_full = attention_weights(query, keys)
    mixture = jnp.einsum(
        "ihqk,ikhd->iqhd", weights_full.astype(low_type), values, preferred_element_type=wide
    )
    return (mixture.reshape(grouped.shape[0], HEADS * HD), weights_full)


def attend_back(grouped, weights_full, grad_mixture):
    query, keys, values = split_heads(grouped)
    images = query.shape[0]
    weights_low = weights_full.astype(low_type)
    grad_out = grad_mixture.reshape(images, SEQ, HEADS, HD)
    grad_weights = jnp.einsum("iqhd,ikhd->ihqk", grad_out, values, preferred_element_type=wide)
    grad_values = jnp.einsum("ihqk,iqhd->ikhd", weights_low, grad_out, preferred_element_type=wide)
    centered = grad_weights - jnp.sum(weights_full * grad_weights, axis=-1, keepdims=True)
    grad_scores = (weights_full * centered).astype(low_type)
    scale = 1.0 / math.sqrt(HD)
    grad_query = jnp.einsum("ihqk,ikhd->iqhd", grad_scores, keys, preferred_element_type=wide)
    grad_keys = jnp.einsum("ihqk,iqhd->ikhd", grad_scores, query, preferred_element_type=wide)
    stacked = jnp.stack([grad_query * scale, grad_keys * scale, grad_values], axis=2)
    return stacked.reshape(images * SEQ, 3 * HEADS * HD)


def adam_step(weight, grad, drift, power, factor, step_value):
    scaled = grad * factor
    new_drift = beta_first * drift + (1.0 - beta_first) * scaled
    new_power = beta_second * power + (1.0 - beta_second) * scaled * scaled
    drift_hat = new_drift / (1.0 - jnp.power(beta_first, step_value))
    power_hat = new_power / (1.0 - jnp.power(beta_second, step_value))
    update = -learn_rate * (drift_hat / (jnp.sqrt(power_hat) + adam_eps) + weight_decay * weight)
    return (update, new_drift, new_power)


def on_device(
    pixels,
    mask_places,
    mask_count,
    targets,
    step_count,
    patch_weight,
    vector_table,
    input_weight,
    output_weight,
    upward_weight,
    downward_weight,
    head_weight,
    drift_patch,
    drift_table,
    drift_input,
    drift_output,
    drift_upward,
    drift_downward,
    drift_head,
    power_patch,
    power_table,
    power_input,
    power_output,
    power_upward,
    power_downward,
    power_head,
):
    rows, cols = (lax.axis_size("row"), lax.axis_size("col"))
    row_index = lax.axis_index("row")
    col_index = lax.axis_index("col")
    images = mask_places.shape[0] // rows
    width = vector_table.shape[1] * rows
    blocks = [
        patch_weight.astype(low_type),
        input_weight[0].astype(low_type).T,
        output_weight[0].astype(low_type),
        upward_weight[0].astype(low_type).T,
        downward_weight[0].astype(low_type),
    ]
    heights = [block.shape[0] for block in blocks]
    gathered = lax.all_gather(jnp.concatenate(blocks, axis=0), BOTH, axis=0, tiled=False)
    gathered = gathered.reshape(rows, cols, sum(heights), -1)

    def whole(index):
        start = sum(heights[:index])
        part = gathered[:, :, start : start + heights[index]]
        return jnp.transpose(part, (1, 2, 0, 3)).reshape(cols * heights[index], width)

    patch_low, input_turned, output_low, upward_turned, downward_low = map(whole, range(5))
    table = lax.all_gather(vector_table, "row", axis=1, tiled=True)
    local_images = pixels.shape[0] // SEQ
    part = pixels.shape[1]
    grid = pixels.reshape(local_images // (rows * images), rows, images, SEQ, part)
    grid = lax.all_to_all(grid, "row", split_axis=1, concat_axis=0, tiled=True)
    grid = grid.reshape(cols, images * SEQ, part)
    grid = lax.all_to_all(grid, "col", split_axis=0, concat_axis=0, tiled=True)
    pixel_own = jnp.transpose(grid, (1, 0, 2)).reshape(images * SEQ, cols * part)

    def own(values):
        return lax.dynamic_slice_in_dim(values, row_index * images, images, axis=0)

    places_own, count_own = (own(mask_places), own(mask_count))

    def gains_of(norm_index):
        return (table[SEQ + 2 + 2 * norm_index], table[SEQ + 3 + 2 * norm_index])

    patch_proj = product(pixel_own, patch_low)
    places = jnp.arange(SEQ, dtype=jnp.int32)
    counted_own = jnp.arange(MSLOT, dtype=jnp.int32)[None, :] < count_own[:, None]
    matches = places_own[:, :, None] == places[None, None, :]
    masked = jnp.any(matches & counted_own[:, :, None], axis=1)[:, :, None]
    opening = (places == 0)[None, :, None]
    stream = jnp.where(
        opening, table[SEQ], jnp.where(masked, table[SEQ + 1], patch_proj.reshape(images, SEQ, -1))
    )
    stream = (stream + table[:SEQ][None]).reshape(images * SEQ, -1)
    gain_one, shift_one = gains_of(0)
    gain_two, shift_two = gains_of(1)
    final_gain, final_shift = gains_of(2)
    normed_one, stats_one = norm_forward(stream, gain_one, shift_one)
    normed_one = normed_one.astype(low_type)
    grouped = product_nt(normed_one, input_turned).astype(low_type)
    mixture, weights_full = attend(grouped)
    mixture = mixture.astype(low_type)
    stream_mid = stream + product(mixture, output_low)
    normed_two, stats_two = norm_forward(stream_mid, gain_two, shift_two)
    normed_two = normed_two.astype(low_type)
    hidden_pre = product_nt(normed_two, upward_turned)
    hidden_act = exact_gelu(hidden_pre).astype(low_type)
    stream_last = stream_mid + product(hidden_act, downward_low)
    final_out, final_stats = norm_forward(stream_last, final_gain, final_shift)
    selector = matches.astype(low_type)
    picked = jnp.einsum(
        "ims,isd->imd",
        selector,
        final_out.astype(low_type).reshape(images, SEQ, -1),
        preferred_element_type=wide,
    ).astype(low_type)
    picked_wide = lax.all_gather(picked.reshape(images * MSLOT, -1), "row", axis=0, tiled=True)
    head_low = head_weight.astype(low_type)
    logits = product(picked_wide, head_low)
    vocab_local = head_weight.shape[1]
    target_local = targets.reshape(-1) - row_index * vocab_local
    target_hits = target_local[:, None] == jnp.arange(vocab_local, dtype=jnp.int32)[None, :]
    chosen = jnp.sum(jnp.where(target_hits, logits, 0.0), axis=1)
    local_top = jnp.max(logits, axis=1)
    local_sum = jnp.sum(jnp.exp(logits - local_top[:, None]), axis=1)
    pair = lax.all_gather(jnp.stack([local_top, local_sum]), "row", axis=0, tiled=False)
    top_value = jnp.max(pair[:, 0], axis=0)
    exp_total = jnp.sum(pair[:, 1] * jnp.exp(pair[:, 0] - top_value), axis=0)
    log_total = top_value + jnp.log(exp_total)
    counted = jnp.arange(MSLOT, dtype=jnp.int32)[None, :] < mask_count[:, None]
    slot_weight = counted.reshape(-1).astype(wide)
    leader_row = (row_index == 0).astype(wide)
    loss_part = jnp.sum(log_total * slot_weight) * leader_row - jnp.sum(chosen * slot_weight)
    count_part = jnp.sum(mask_count.astype(wide)) * leader_row
    grad_logits = (
        (jnp.exp(logits - log_total[:, None]) - target_hits.astype(wide)) * slot_weight[:, None]
    ).astype(low_type)
    grad_head_local = product_tn(picked_wide, grad_logits)
    grad_head = lax.psum(grad_head_local.astype(low_type), "col").astype(wide)
    grad_picked = lax.psum_scatter(
        product_nt(grad_logits, head_low).astype(low_type), "row", scatter_dimension=0, tiled=True
    )
    grad_final = jnp.einsum(
        "ims,imd->isd",
        selector,
        grad_picked.reshape(images, MSLOT, -1),
        preferred_element_type=wide,
    )
    grad_stream, grad_final_gain, grad_final_shift = norm_backward(
        grad_final.reshape(images * SEQ, -1), final_stats, final_gain
    )
    grad_two = grad_stream.astype(low_type)
    grad_downward = product_tn(hidden_act, grad_two)
    grad_act = product_nt(grad_two, downward_low)
    _, gelu_pull = jax.vjp(exact_gelu, hidden_pre)
    grad_pre = gelu_pull(grad_act)[0].astype(low_type)
    grad_upward_turned = product_tn(grad_pre, normed_two)
    grad_normed_two = product(grad_pre, upward_turned)
    grad_mid, grad_gain_two, grad_shift_two = norm_backward(grad_normed_two, stats_two, gain_two)
    grad_mid = grad_mid + grad_stream
    grad_one = grad_mid.astype(low_type)
    grad_output = product_tn(mixture, grad_one)
    grad_mixture = product_nt(grad_one, output_low).astype(low_type)
    grad_grouped = attend_back(grouped, weights_full, grad_mixture).astype(low_type)
    grad_input_turned = product_tn(grad_grouped, normed_one)
    grad_normed_one = product(grad_grouped, input_turned)
    grad_below, grad_gain_one, grad_shift_one = norm_backward(grad_normed_one, stats_one, gain_one)
    grad_grid = (grad_below + grad_mid).reshape(images, SEQ, -1)
    grad_patch = jnp.where(opening | masked, 0.0, grad_grid).reshape(images * SEQ, -1)
    grad_patch_weight = product_tn(pixel_own, grad_patch.astype(low_type))
    lines = [
        jnp.sum(grad_grid, axis=0),
        jnp.sum(grad_grid[:, 0], axis=0)[None],
        jnp.sum(jnp.where(masked, grad_grid, 0.0), axis=(0, 1))[None],
        jnp.stack(
            [
                grad_gain_one,
                grad_shift_one,
                grad_gain_two,
                grad_shift_two,
                grad_final_gain,
                grad_final_shift,
            ]
        ),
    ]
    table_local = jnp.concatenate(lines, axis=0).astype(low_type)

    def dealt(value, height):
        grid = value.astype(low_type).reshape(cols, height, rows, -1)
        return jnp.transpose(grid, (2, 0, 1, 3)).reshape(rows * cols, height, -1)

    stacked = jnp.concatenate(
        [
            dealt(value, height)
            for value, height in zip(
                [
                    grad_patch_weight,
                    grad_input_turned,
                    grad_output,
                    grad_upward_turned,
                    grad_downward,
                ],
                heights,
            )
        ],
        axis=1,
    )
    summed = lax.psum_scatter(stacked, BOTH, scatter_dimension=0, tiled=False).astype(wide)
    starts = [sum(heights[:index]) for index in range(6)]
    pieces = [summed[starts[index] : starts[index + 1]] for index in range(5)]
    grad_table = lax.psum(table_local, BOTH).astype(wide)
    grad_table = lax.dynamic_slice_in_dim(
        grad_table, row_index * vector_table.shape[1], vector_table.shape[1], axis=1
    )
    leader_col = (col_index == 0).astype(wide)
    squares_part = jnp.sum(summed * summed) + leader_col * (
        jnp.sum(grad_table * grad_table) + jnp.sum(grad_head * grad_head)
    )
    loss_total, count_total, squares_total = lax.psum((loss_part, count_part, squares_part), BOTH)
    mean_loss = loss_total / count_total
    grad_norm = jnp.sqrt(squares_total) / count_total
    factor = jnp.minimum(1.0, clip_limit / grad_norm) / count_total
    step_value = step_count[0].astype(wide)
    steps = [
        (patch_weight, pieces[0], drift_patch, power_patch),
        (vector_table, grad_table, drift_table, power_table),
        (input_weight, pieces[1].T[None], drift_input, power_input),
        (output_weight, pieces[2][None], drift_output, power_output),
        (upward_weight, pieces[3].T[None], drift_upward, power_upward),
        (downward_weight, pieces[4][None], drift_downward, power_downward),
        (head_weight, grad_head, drift_head, power_head),
    ]
    results = []
    for weight, grad, drift, power in steps:
        results.extend(adam_step(weight, grad, drift, power, factor, step_value))
    return (mean_loss, grad_norm, *results)


def solution(mesh):
    state = (
        P("col", "row"),
        P(None, "row"),
        P(None, "row", "col"),
        P(None, "col", "row"),
        P(None, "row", "col"),
        P(None, "col", "row"),
        P(None, "row"),
    )
    data = (P("row", "col"), P("col", None), P("col"), P("col", None), P())
    outs = (P(), P()) + tuple((spec for spec in state for _ in range(3)))
    return jax.shard_map(
        on_device, mesh=mesh, in_specs=data + state * 3, out_specs=outs, check_vma=False
    )
```

profile of v0, /device:TPU:0, one launch (start us, length us, event | category | flops | bytes accessed | tf_op | source)
XLA Modules:
  0.0 804.0 jit_solution(17140014691448463150)
XLA Ops:
  12.9 2.2 reshape.609
  15.8 4.2 all-to-all-start
  21.4 16.2 %all_gather.18 = f32[205,768]{1,0:T(8,128)S(1)} all-gather(f32[205,384]{1,0:T(8,128)S(1)} %copy-done.33), channel_id=1, replica_groups=mesh['row'=2,'col'=16] {'row'}, dimensions={1}, use_global_device_ids=true | all-gather | bytes 944640 | tf_op jit(solution)/shard_map/all_gather | solution.py:154
  38.8 6.1 all-to-all-start.1
  45.0 86.4 %all-gather.5.cloned.1.call-done = bf16[19968,384]{1,0:T(8,128)(2,1)} async-done(((bf16[624,384]{1,0:T(8,128)(2,1)}), bf16[19968,384]{1,0:T(8,128)(2,1)}) %all-gather.5.cloned.1.call-update) | async-done | bytes 15335440 | tf_op jit(solution)/shard_map/all_gather | solution.py:145
  131.4 2.9 fusion.86
  134.3 2.4 slice.116
  138.1 3.6 copy.146
  141.7 2.4 copy.152
  144.1 8.6 %fusion.85 = (bf16[2,16,192,384]{3,2,1,0:T(8,128)(2,1)}, bf16[2,16,192,384]{3,2,1,0:T(8,128)(2,1)}) fusion(bf16[2,16,624,384]{3,2,1,0:T(8,128)(2,1)} %bitcast.239), kind=kLoop, calls=%fused_computation.207 | loop fusion | bytes 18874368 | tf_op jit(solution)/shard_map/slice | solution.py:150
  155.3 3.3 convolution_convert_fusion.4
  161.9 2.1 fusion.89
  165.5 9.8 %copy.148 = bf16[2,16,192,384]{3,0,2,1:T(2,128)(2,1)} copy(bf16[2,16,192,384]{3,2,1,0:T(8,128)(2,1)} %get-tuple-element.77) | data formatting | bytes 9437184
  175.3 5.5 copy.154
  183.0 9.8 %copy.149 = bf16[2,16,192,384]{3,0,2,1:T(2,128)(2,1)} copy(bf16[2,16,192,384]{3,2,1,0:T(8,128)(2,1)} %get-tuple-element.76) | data formatting | bytes 9437184
  192.8 3.1 copy.155
  196.0 11.2 %multiply_convert_fusion.2 = (bf16[197,3072]{1,0:T(8,128)(2,1)S(1)}, f32[197,3072]{1,0:T(8,128)}, f32[197,3072]{1,0:T(8,128)}) fusion(bf16[3072,768]{1,0:T(8,128)(2,1)} %bitcast.254, f32[197,768]{1,0:T(8,128)S(1)} %get-tuple-element.88, f32[768]{0:T(1024)S(1)} %get-tuple-element.33, f32[768]{0:T(1024)S(1)} %get-tuple-element.34, ...), kind=kOutput, calls=%fused_computation.27 | convolution fusion | flops 969656064 | bytes 11383336 | tf_op jit(solution)/shard_map/ab,cb->ac/dot_general | solution.py:28
  209.2 6.1 all_gather.21
  217.7 4.5 all-gather.2
  222.9 3.1 fusion.25
  226.1 9.8 %reduce-scatter.3.cloned.1.call-done = bf16[80,768]{1,0:T(8,128)(2,1)} async-done(((bf16[160,768]{1,0:T(8,128)(2,1)}), bf16[80,768]{1,0:T(8,128)(2,1)}) %reduce-scatter.3.cloned.1.call-update) | async-done | bytes 122896 | tf_op jit(solution)/shard_map/reduce_scatter | solution.py:226
  235.9 2.4 multiply_reduce_fusion.3
  239.8 5.3 add_convert_fusion
  245.2 1.9 multiply_reduce_fusion.4
  249.9 2.4 convolution_bitcast_fusion
  263.1 4.1 concatenate.18
  267.2 5.7 convolution_convert_fusion
  276.4 2.5 copy.135
  278.9 3.0 convolution_convert_fusion.3
  281.9 7.9 reshape.623
  289.8 4.3 copy.136
  295.8 2.6 copy.137
  298.5 3.8 convolution_convert_fusion.2
  302.3 10.1 %reshape.627 = bf16[16,192,2,384]{3,2,1,0:T(2,128)(2,1)} reshape(bf16[3072,768]{1,0:T(8,128)(2,1)} %convolution_convert_fusion.2) | data formatting | bytes 9437184 | tf_op jit(solution)/shard_map/reshape | solution.py:275
  312.4 5.6 copy.138
  318.0 3.7 convolution_convert_fusion.1
  321.7 10.3 %reshape.629 = bf16[16,192,2,384]{3,2,1,0:T(2,128)(2,1)} reshape(bf16[3072,768]{1,0:T(8,128)(2,1)} %convolution_convert_fusion.1) | data formatting | bytes 9437184 | tf_op jit(solution)/shard_map/reshape | solution.py:275
  332.0 3.5 copy.139
  336.7 2.2 constant_dynamic-update-slice_fusion.3
  341.0 2.7 constant_dynamic-update-slice_fusion.1
  343.7 2.7 constant_dynamic-update-slice_fusion
  349.7 43.2 %all-reduce.4.cloned.1.call-done = bf16[205,768]{1,0:T(8,128)(2,1)} async-done(((bf16[205,768]{1,0:T(8,128)(2,1)}), bf16[205,768]{1,0:T(8,128)(2,1)}) %all-reduce.4.cloned.1.call-update) | async-done | bytes 314896 | tf_op jit(solution)/shard_map/psum | solution.py:297
  394.6 142.9 %all-reduce.6.cloned.1.call-done = bf16[768,4096]{1,0:T(8,128)(2,1)} async-done(((bf16[768,4096]{1,0:T(8,128)(2,1)}), bf16[768,4096]{1,0:T(8,128)(2,1)}) %all-reduce.6.cloned.1.call-update) | async-done | bytes 6291472 | tf_op jit(solution)/shard_map/psum | solution.py:225
  537.5 6.6 fusion.3
  545.6 166.7 %reduce-scatter.5.cloned.1.call-done = bf16[1,624,384]{2,1,0:T(8,128)(2,1)} async-done(((bf16[32,624,384]{2,1,0:T(8,128)(2,1)}), bf16[1,624,384]{2,1,0:T(8,128)(2,1)}) %reduce-scatter.5.cloned.1.call-update) | async-done | bytes 479248 | tf_op jit(solution)/shard_map/reduce_scatter | solution.py:294
  712.3 1.9 multiply_reduce_fusion.2
  714.8 39.5 %all-reduce = (f32[]{:T(128)}, f32[]{:T(128)}, f32[]{:T(128)}) all-reduce(f32[]{:T(128)S(6)} %sub.160, f32[]{:T(128)S(6)} %mul.642, f32[]{:T(128)S(6)} %add.237), channel_id=1, replica_groups=mesh['row'=2,'col'=16] {'row','col'}, use_global_device_ids=true, to_apply=%region_16.17 | all-reduce | flops 3 | bytes 24 | tf_op jit(solution)/shard_map/psum | solution.py:305
  765.2 29.5 %add_multiply_fusion = (f32[768,4096]{1,0:T(8,128)}, f32[768,4096]{1,0:T(8,128)}, f32[768,4096]{1,0:T(8,128)}) fusion(f32[768,4096]{1,0:T(8,128)} %param.37, f32[]{:T(128)} %bitcast.60, f32[]{:T(128)} %bitcast.59, f32[]{:T(128)S(6)} %div.165, bf16[768,4096]{1,0:T(8,128)(2,1)} %all-reduce.6.cloned.1.call-done, f32[768,4096]{1,0:T(8,128)} %param.51, ...), kind=kLoop, calls=%fused_computation.8 | loop fusion | flops 50331648 | bytes 81788944 | tf_op jit(solution)/shard_map/mul | solution.py:100
  (284 shorter events, 57.3 us)
Async XLA Ops:
  7.2 13.5 %copy-start = (s32[2,80]{1,0:T(2,128)S(1)}, s32[2,80]{1,0:T(2,128)}, u32[]{:S(2)}) copy-start(s32[2,80]{1,0:T(2,128)} %param.27) | copy-start | bytes 1924
  7.2 12.9 %copy-start.82 = (s32[2]{0:T(128)S(1)}, s32[2]{0:T(128)}, u32[]{:S(2)}) copy-start(s32[2]{0:T(128)} %param.28) | copy-start | bytes 28
  7.2 14.2 %copy-start.33 = (f32[205,384]{1,0:T(8,128)S(1)}, f32[205,384]{1,0:T(8,128)}, u32[]{:S(2)}) copy-start(f32[205,384]{1,0:T(8,128)} %param.32) | copy-start | bytes 944644
  7.2 124.2 %all-gather.5.cloned.1.call-start = ((), (), s32[]{:S(2)}) async-start(), calls=%async_computation.8 | async-start | bytes 15814656 | tf_op jit(solution)/shard_map/all_gather | solution.py:145
  8.2 29.5 %copy-start.78 = (s32[2,80]{1,0:T(2,128)S(1)}, s32[2,80]{1,0:T(2,128)}, u32[]{:S(2)}) copy-start(s32[2,80]{1,0:T(2,128)} %param.29) | copy-start | bytes 1924
  15.8 22.2 %all-to-all-start = ((bf16[8,2,1,197,48]{3,0,4,2,1:T(8,128)(2,1)}), bf16[8,2,1,197,48]{3,0,4,2,1:T(8,128)(2,1)S(1)}, u32[]{:S(2)}, u32[]{:S(2)}) async-start(bf16[8,2,1,197,48]{3,0,4,2,1:T(8,128)(2,1)} %copy.121), calls=%async_computation | async-start | bytes 786432 | tf_op jit(solution)/shard_map/all_to_all | solution.py:158
  21.4 132.0 %copy-start.79 = (pred[197]{0:T(512)(128)(4,1)}, pred[197]{0:T(512)(128)(4,1)S(1)}, u32[]{:S(2)}) copy-start(pred[197]{0:T(512)(128)(4,1)S(1)} %fusion.60) | copy-start | bytes 595
  37.6 93.8 %copy-start.38 = (f32[205,768]{1,0:T(8,128)}, f32[205,768]{1,0:T(8,128)S(1)}, u32[]{:S(2)}) copy-start(f32[205,768]{1,0:T(8,128)S(1)} %all_gather.18) | copy-start | bytes 1889284
  37.9 185.0 %copy-start.62 = (s32[160]{0:T(256)}, s32[160]{0:T(256)S(1)}, u32[]{:S(2)}) copy-start(s32[160]{0:T(256)S(1)} %sub.159) | copy-start | bytes 1924
  37.9 185.0 %copy-start.73 = (f32[160]{0:T(256)}, f32[160]{0:T(256)S(1)}, u32[]{:S(2)}) copy-start(f32[160]{0:T(256)S(1)} %convert_element_type.195) | copy-start | bytes 1924
  38.0 158.0 %copy-start.65 = (f32[768]{0:T(1024)}, f32[768]{0:T(1024)S(1)}, u32[]{:S(2)}) copy-start(f32[768]{0:T(1024)S(1)} %get-tuple-element.33) | copy-start | bytes 9220
  38.8 113.9 %all-to-all-start.1 = ((bf16[16,197,48]{1,2,0:T(8,128)(2,1)}), bf16[16,197,48]{1,2,0:T(8,128)(2,1)S(1)}, u32[]{:S(2)}, u32[]{:S(2)}) async-start(bf16[16,197,48]{1,2,0:T(8,128)(2,1)} %bitcast.12), calls=%async_computation.1 | async-start | bytes 786432 | tf_op jit(solution)/shard_map/all_to_all | solution.py:160
  45.0 190.9 %reduce-scatter.3.cloned.1.call-start = ((), (), s32[]{:S(2)}) async-start(), calls=%async_computation.4 | async-start | bytes 368640 | tf_op jit(solution)/shard_map/reduce_scatter | solution.py:226
  144.1 9.3 %copy-start.39 = (f32[205,768]{1,0:T(8,128)S(1)}, f32[205,768]{1,0:T(8,128)}, u32[]{:S(2)}) copy-start(f32[205,768]{1,0:T(8,128)} %copy-done.38) | copy-start | bytes 1889284
  164.0 16.8 %copy-start.57 = (f32[12,197]{1,0:T(8,128)}, f32[12,197]{1,0:T(8,128)S(1)}, u32[]{:S(2)}) copy-start(f32[12,197]{1,0:T(8,128)S(1)} %get-tuple-element.85) | copy-start | bytes 28372
  165.5 16.7 %copy-start.8 = (bf16[96,8,2,384]{3,1,2,0:T(8,128)(2,1)}, bf16[96,8,2,384]{3,1,2,0:T(8,128)(2,1)S(1)}, u32[]{:S(2)}) copy-start(bf16[96,8,2,384]{3,1,2,0:T(8,128)(2,1)S(1)} %copy.153) | copy-start | bytes 3538948
  175.3 5.5 copy-start.10
  182.2 10.6 %copy-start.31 = (bf16[12,64,197]{2,1,0:T(8,128)(2,1)}, bf16[12,64,197]{2,1,0:T(8,128)(2,1)S(1)}, u32[]{:S(2)}) copy-start(bf16[12,64,197]{2,1,0:T(8,128)(2,1)S(1)} %convolution_convert_fusion.7) | copy-start | bytes 907780
  182.7 24.4 %copy-start.3 = (f32[197,768]{1,0:T(8,128)}, f32[197,768]{1,0:T(8,128)S(1)}, u32[]{:S(2)}) copy-start(f32[197,768]{1,0:T(8,128)S(1)} %get-tuple-element.88) | copy-start | bytes 1815556
  182.7 64.3 %copy-start.63 = (f32[197]{0:T(256)}, f32[197]{0:T(256)S(1)}, u32[]{:S(2)}) copy-start(f32[197]{0:T(256)S(1)} %broadcast_multiply_fusion.7) | copy-start | bytes 2368
  183.0 64.1 %copy-start.70 = (f32[197]{0:T(256)}, f32[197]{0:T(256)S(1)}, u32[]{:S(2)}) copy-start(f32[197]{0:T(256)S(1)} %add_rsqrt_fusion.1) | copy-start | bytes 2368
  195.9 11.2 %copy-start.2 = (bf16[384,8,2,384]{3,1,2,0:T(8,128)(2,1)}, bf16[384,8,2,384]{3,1,2,0:T(8,128)(2,1)S(1)}, u32[]{:S(2)}) copy-start(bf16[384,8,2,384]{3,1,2,0:T(8,128)(2,1)S(1)} %copy.155) | copy-start | bytes 14155780
  195.9 19.5 %slice-start = ((s8[12582912]{0:T(1024)(128)(4,1)}), s8[4194304]{0:T(1024)(128)(4,1)S(1)}, s32[]{:S(2)}) async-start(s8[12582912]{0:T(1024)(128)(4,1)} %bitcast.225), calls=%async_computation.9 | async-start | bytes 8388608
  195.9 19.5 %slice-start.1 = ((s8[12582912]{0:T(1024)(128)(4,1)}), s8[4194304]{0:T(1024)(128)(4,1)S(1)}, s32[]{:S(2)}) async-start(s8[12582912]{0:T(1024)(128)(4,1)} %bitcast.225), calls=%async_computation.10 | async-start | bytes 8388608
  196.0 19.4 %slice-start.2 = ((s8[12582912]{0:T(1024)(128)(4,1)}), s8[4194304]{0:T(1024)(128)(4,1)S(1)}, s32[]{:S(2)}) async-start(s8[12582912]{0:T(1024)(128)(4,1)} %bitcast.225), calls=%async_computation.11 | async-start | bytes 8388608
  226.1 166.9 %all-reduce.4.cloned.1.call-start = ((), (), s32[]{:S(2)}) async-start(), calls=%async_computation.6 | async-start | bytes 638976 | tf_op jit(solution)/shard_map/psum | solution.py:297
  238.3 6.8 slice-start.5
  239.7 7.3 copy-start.21
  239.8 5.4 copy-start.4
  239.8 5.4 slice-start.6
  256.9 5.6 copy-start.74
  267.2 270.3 %all-reduce.6.cloned.1.call-start = ((), (), s32[]{:S(2)}) async-start(), calls=%async_computation.7 | async-start | bytes 12582912 | tf_op jit(solution)/shard_map/psum | solution.py:225
  272.9 439.4 %reduce-scatter.5.cloned.1.call-start = ((), (), s32[]{:S(2)}) async-start(), calls=%async_computation.5 | async-start | bytes 15814656 | tf_op jit(solution)/shard_map/reduce_scatter | solution.py:294
  312.4 5.6 copy-start.19
  312.4 5.6 copy-start.22
  394.5 365.0 %copy-start.45 = (f32[48,384]{1,0:T(8,128)S(1)}, f32[48,384]{1,0:T(8,128)}, u32[]{:S(2)}) copy-start(f32[48,384]{1,0:T(8,128)} %param.31) | copy-start | bytes 221188
  394.5 365.0 %copy-start.53 = (f32[48,384]{1,0:T(8,128)S(1)}, f32[48,384]{1,0:T(8,128)}, u32[]{:S(2)}) copy-start(f32[48,384]{1,0:T(8,128)} %param.45) | copy-start | bytes 221188
  394.6 365.1 %copy-start.54 = (f32[48,384]{1,0:T(8,128)S(1)}, f32[48,384]{1,0:T(8,128)}, u32[]{:S(2)}) copy-start(f32[48,384]{1,0:T(8,128)} %param.38) | copy-start | bytes 221188
  544.1 216.2 %copy-start.37 = (f32[1,384,144]{1,2,0:T(8,128)S(1)}, f32[1,384,144]{1,2,0:T(8,128)}, u32[]{:S(2)}) copy-start(f32[1,384,144]{1,2,0:T(8,128)} %param.33) | copy-start | bytes 663556
  544.1 216.2 %copy-start.51 = (f32[1,384,144]{1,2,0:T(8,128)S(1)}, f32[1,384,144]{1,2,0:T(8,128)}, u32[]{:S(2)}) copy-start(f32[1,384,144]{1,2,0:T(8,128)} %param.47) | copy-start | bytes 663556
  544.1 216.2 %copy-start.52 = (f32[1,384,144]{1,2,0:T(8,128)S(1)}, f32[1,384,144]{1,2,0:T(8,128)}, u32[]{:S(2)}) copy-start(f32[1,384,144]{1,2,0:T(8,128)} %param.40) | copy-start | bytes 663556
  544.1 217.1 %copy-start.46 = (f32[1,48,384]{2,1,0:T(8,128)S(1)}, f32[1,48,384]{2,1,0:T(8,128)}, u32[]{:S(2)}) copy-start(f32[1,48,384]{2,1,0:T(8,128)} %param.34) | copy-start | bytes 221188
  544.1 217.1 %copy-start.55 = (f32[1,48,384]{2,1,0:T(8,128)S(1)}, f32[1,48,384]{2,1,0:T(8,128)}, u32[]{:S(2)}) copy-start(f32[1,48,384]{2,1,0:T(8,128)} %param.48) | copy-start | bytes 221188
  544.1 217.1 %copy-start.56 = (f32[1,48,384]{2,1,0:T(8,128)S(1)}, f32[1,48,384]{2,1,0:T(8,128)}, u32[]{:S(2)}) copy-start(f32[1,48,384]{2,1,0:T(8,128)} %param.41) | copy-start | bytes 221188
  544.1 217.9 %copy-start.35 = (f32[1,384,192]{1,2,0:T(8,128)S(1)}, f32[1,384,192]{1,2,0:T(8,128)}, u32[]{:S(2)}) copy-start(f32[1,384,192]{1,2,0:T(8,128)} %param.35) | copy-start | bytes 884740
  544.1 217.9 %copy-start.47 = (f32[1,384,192]{1,2,0:T(8,128)S(1)}, f32[1,384,192]{1,2,0:T(8,128)}, u32[]{:S(2)}) copy-start(f32[1,384,192]{1,2,0:T(8,128)} %param.49) | copy-start | bytes 884740
  544.2 217.9 %copy-start.48 = (f32[1,384,192]{1,2,0:T(8,128)S(1)}, f32[1,384,192]{1,2,0:T(8,128)}, u32[]{:S(2)}) copy-start(f32[1,384,192]{1,2,0:T(8,128)} %param.42) | copy-start | bytes 884740
  765.2 29.5 %copy-start.1 = (s32[2,80]{1,0:T(2,128)S(1)}, s32[2,80]{1,0:T(2,128)}, u32[]{:S(2)}) copy-start(s32[2,80]{1,0:T(2,128)} %param.27) | copy-start | bytes 1924
  (51 other events, 143.8 us)
Sparse Core Ops, SparseCore 0:
  13.0 118.3 all-gather.4
  226.2 9.6 reduce-scatter.2
  267.3 125.5 all-reduce.3
  397.4 139.9 all-reduce.5
  543.5 168.7 reduce-scatter.4
where the time goes:
time: 814 us; the launch traced here: 804 us
  waiting for transfers between devices  449 us (55%)
  local copies, waits for them, and re-layouts  134 us (16%)
  blocking collectives  66.4 us (8%)
  other arithmetic  59.5 us (7%)
  matrix products  58.2 us (7%)
  between operations  26.4 us (3%)
  starting transfers between devices  10.8 us (1%)
    reduce_scatter x1, waiting for transfers between devices, on_device(): lax.psum_scatter(stacked, BOTH, scatter_dimension=0, tiled=False)  167 us
    psum x1, waiting for transfers between devices, on_device(): grad_head = lax.psum(grad_head_local.astype(low_type), 'col').astype(wide)  143 us
    all_gather x1, waiting for transfers between devices, on_device(): lax.all_gather(jnp.concatenate(blocks, axis=0), BOTH, axis=0, tiled=False)  86.4 us
    unnamed x198, local copies, waits for them, and re-layouts  51.5 us
    psum x1, waiting for transfers between devices, on_device(): grad_table = lax.psum(table_local, BOTH).astype(wide)  43.2 us
    psum x1, blocking collectives, on_device(): lax.psum((loss_part, count_part, squares_part), BOTH)  39.5 us
    mul x7, other arithmetic, adam_step(): -learn_rate  35 us
    reshape x5, local copies, waits for them, and re-layouts, dealt(): grid = value.astype(low_type).reshape(cols, height, rows, -1)  30.7 us
  transfers between devices with their start and end apart: 7, of which 5 were waited for; matrix products, arithmetic and copies ran while one was open for 14% of the time, Pallas kernels for 0%

commit v1 on v0

--- a/solution.py
+++ b/solution.py
@@ -294,7 +294,7 @@
     summed = lax.psum_scatter(stacked, BOTH, scatter_dimension=0, tiled=False).astype(wide)
     starts = [sum(heights[:index]) for index in range(6)]
     pieces = [summed[starts[index] : starts[index + 1]] for index in range(5)]
-    grad_table = lax.psum(table_local, BOTH).astype(wide)
+    grad_table = lax.psum(lax.psum(table_local, "col"), "row").astype(wide)
     grad_table = lax.dynamic_slice_in_dim(
         grad_table, row_index * vector_table.shape[1], vector_table.shape[1], axis=1
     )

time: 814 us -> 707 us (0.87)
  waiting for transfers between devices: 449 us -> 358 us
  local copies, waits for them, and re-layouts: 134 us -> 121 us
    psum x2, waiting for transfers between devices: 186 us -> 100 us  [on_device(): grad_table = lax.psum(lax.psum(table_local, 'col'), 'row').astype(wide)]
    unnamed x198 -> x178, local copies, waits for them, and re-layouts: 51.5 us -> 55.7 us
  transfers between devices with their start and end apart: 7 -> 7, of which waited for: 5 -> 4; matrix products, arithmetic and copies ran while one was open for 14% -> 15% of each run, Pallas kernels for 0% -> 0%
where the time goes in v1:
time: 707 us; the launch traced here: 697 us
  waiting for transfers between devices  358 us (51%)
  local copies, waits for them, and re-layouts  121 us (17%)
  blocking collectives  66.4 us (9%)
  other arithmetic  59.9 us (8%)
  matrix products  54.4 us (8%)
  between operations  26.3 us (4%)
  starting transfers between devices  11 us (2%)
    reduce_scatter x1, waiting for transfers between devices, on_device(): lax.psum_scatter(stacked, BOTH, scatter_dimension=0, tiled=False)  166 us
    psum x2, waiting for transfers between devices, on_device(): grad_table = lax.psum(lax.psum(table_local, 'col'), 'row').astype(wide)  100 us
    all_gather x1, waiting for transfers between devices, on_device(): lax.all_gather(jnp.concatenate(blocks, axis=0), BOTH, axis=0, tiled=False)  86.4 us
    unnamed x178, local copies, waits for them, and re-layouts  55.7 us
    psum x1, blocking collectives, on_device(): lax.psum((loss_part, count_part, squares_part), BOTH)  39.5 us
    mul x7, other arithmetic, adam_step(): -learn_rate  35.2 us
    dot_general x5, matrix products, product_nt(): return jnp.einsum('ab,cb->ac', left, right, preferred_element_type=wide)  24.5 us
    reshape x5, local copies, waits for them, and re-layouts, dealt(): grid = value.astype(low_type).reshape(cols, height, rows, -1)  23.9 us
  transfers between devices with their start and end apart: 7, of which 4 were waited for; matrix products, arithmetic and copies ran while one was open for 15% of the time, Pallas kernels for 0%

profile of v1, /device:TPU:0, one launch (start us, length us, event | category | flops | bytes accessed | tf_op | source)
XLA Modules:
  0.0 697.4 jit_solution(5355580022647944951)
XLA Ops:
  12.9 2.2 reshape.609
  15.8 4.2 all-to-all-start
  21.4 16.2 %all_gather.18 = f32[205,768]{1,0:T(8,128)S(1)} all-gather(f32[205,384]{1,0:T(8,128)S(1)} %copy-done.33), channel_id=1, replica_groups=mesh['row'=2,'col'=16] {'row'}, dimensions={1}, use_global_device_ids=true | all-gather | bytes 944640 | tf_op jit(solution)/shard_map/all_gather | solution.py:154
  39.3 6.1 all-to-all-start.1
  45.5 86.4 %all-gather.5.cloned.1.call-done = bf16[19968,384]{1,0:T(8,128)(2,1)} async-done(((bf16[624,384]{1,0:T(8,128)(2,1)}), bf16[19968,384]{1,0:T(8,128)(2,1)}) %all-gather.5.cloned.1.call-update) | async-done | bytes 15335440 | tf_op jit(solution)/shard_map/all_gather | solution.py:145
  131.9 1.9 fusion.86
  133.8 2.4 slice.116
  138.6 3.6 copy.146
  142.3 2.4 copy.152
  144.7 8.6 %fusion.85 = (bf16[2,16,192,384]{3,2,1,0:T(8,128)(2,1)}, bf16[2,16,192,384]{3,2,1,0:T(8,128)(2,1)}) fusion(bf16[2,16,624,384]{3,2,1,0:T(8,128)(2,1)} %bitcast.237), kind=kLoop, calls=%fused_computation.207 | loop fusion | bytes 18874368 | tf_op jit(solution)/shard_map/slice | solution.py:150
  153.3 2.0 fusion.88
  155.6 4.3 convolution_convert_fusion.4
  159.8 1.7 copy.124
  162.1 2.1 fusion.89
  165.7 9.8 %copy.148 = bf16[2,16,192,384]{3,0,2,1:T(2,128)(2,1)} copy(bf16[2,16,192,384]{3,2,1,0:T(8,128)(2,1)} %get-tuple-element.79) | data formatting | bytes 9437184
  175.5 5.5 copy.154
  183.2 9.8 %copy.149 = bf16[2,16,192,384]{3,0,2,1:T(2,128)(2,1)} copy(bf16[2,16,192,384]{3,2,1,0:T(8,128)(2,1)} %get-tuple-element.78) | data formatting | bytes 9437184
  193.0 3.1 copy.155
  196.2 11.2 %multiply_convert_fusion.2 = (bf16[197,3072]{1,0:T(8,128)(2,1)S(1)}, f32[197,3072]{1,0:T(8,128)}, f32[197,3072]{1,0:T(8,128)}) fusion(bf16[3072,768]{1,0:T(8,128)(2,1)} %bitcast.252, f32[197,768]{1,0:T(8,128)S(1)} %get-tuple-element.90, f32[768]{0:T(1024)S(1)} %get-tuple-element.33, f32[768]{0:T(1024)S(1)} %get-tuple-element.34, ...), kind=kOutput, calls=%fused_computation.27 | convolution fusion | flops 969656064 | bytes 11383336 | tf_op jit(solution)/shard_map/ab,cb->ac/dot_general | solution.py:28
  209.5 6.1 all_gather.21
  218.1 4.5 all-gather.2
  223.3 3.2 fusion.25
  226.5 4.7 convolution_convert_fusion
  231.2 5.0 reduce-scatter.3.cloned.1.call-done
  236.3 1.7 multiply_reduce_fusion.3
  239.5 5.3 add_convert_fusion
  248.9 1.6 convolution_bitcast_fusion
  252.8 1.8 copy-done.9
  256.2 3.3 concatenate.18
  264.0 1.9 convolution_convert_fusion.3
  265.9 3.1 reshape.623
  269.0 4.4 copy.136
  275.6 3.8 convolution_convert_fusion.2
  279.4 10.1 %reshape.627 = bf16[16,192,2,384]{3,2,1,0:T(2,128)(2,1)} reshape(bf16[3072,768]{1,0:T(8,128)(2,1)} %convolution_convert_fusion.2) | data formatting | bytes 9437184 | tf_op jit(solution)/shard_map/reshape | solution.py:275
  289.5 5.7 copy.138
  296.4 2.2 constant_dynamic-update-slice_fusion.3
  300.5 3.7 convolution_convert_fusion.1
  304.2 100.3 %all-reduce.7.cloned.1.call-done = (bf16[205,768]{1,0:T(8,128)(2,1)}, bf16[768,4096]{1,0:T(8,128)(2,1)}) async-done(((bf16[205,768]{1,0:T(8,128)(2,1)}, bf16[768,4096]{1,0:T(8,128)(2,1)}), (bf16[205,768]{1,0:T(8,128)(2,1)}, bf16[768,4096]{1,0:T(8,128)(2,1)})) %all-reduce.7.cloned.1.call-update) | async-done | bytes 6606352 | tf_op jit(solution)/shard_map/psum | solution.py:297
  404.9 5.0 constant_dynamic-update-slice_fusion.1
  409.9 10.1 %reshape.629 = bf16[16,192,2,384]{3,2,1,0:T(2,128)(2,1)} reshape(bf16[3072,768]{1,0:T(8,128)(2,1)} %convolution_convert_fusion.1) | data formatting | bytes 9437184 | tf_op jit(solution)/shard_map/reshape | solution.py:275
  420.0 3.3 copy.139
  423.3 2.6 constant_dynamic-update-slice_fusion
  429.3 6.7 fusion.3
  436.1 1.8 fusion.34
  439.1 166.5 %reduce-scatter.5.cloned.1.call-done = bf16[1,624,384]{2,1,0:T(8,128)(2,1)} async-done(((bf16[32,624,384]{2,1,0:T(8,128)(2,1)}), bf16[1,624,384]{2,1,0:T(8,128)(2,1)}) %reduce-scatter.5.cloned.1.call-update) | async-done | bytes 479248 | tf_op jit(solution)/shard_map/reduce_scatter | solution.py:294
  605.6 1.9 multiply_reduce_fusion.2
  608.1 39.5 %all-reduce = (f32[]{:T(128)}, f32[]{:T(128)}, f32[]{:T(128)}) all-reduce(f32[]{:T(128)S(6)} %sub.160, f32[]{:T(128)S(6)} %mul.642, f32[]{:T(128)S(6)} %add.239), channel_id=1, replica_groups=mesh['row'=2,'col'=16] {'row','col'}, use_global_device_ids=true, to_apply=%region_16.17 | all-reduce | flops 3 | bytes 24 | tf_op jit(solution)/shard_map/psum | solution.py:305
  657.4 29.6 %add_multiply_fusion = (f32[768,4096]{1,0:T(8,128)}, f32[768,4096]{1,0:T(8,128)}, f32[768,4096]{1,0:T(8,128)}) fusion(f32[768,4096]{1,0:T(8,128)} %param.37, f32[]{:T(128)} %bitcast.60, f32[]{:T(128)} %bitcast.59, f32[]{:T(128)S(6)} %div.165, bf16[768,4096]{1,0:T(8,128)(2,1)} %get-tuple-element.51, f32[768,4096]{1,0:T(8,128)} %param.51, f32[768,4096]{1,0:T(8,128)} %param.44), kind=kLoop, calls=%fused_computation.8 | loop fusion | flops 50331648 | bytes 81788944 | tf_op jit(solution)/shard_map/mul | solution.py:100
  (263 shorter events, 48.1 us)
Async XLA Ops:
  7.2 13.5 %copy-start = (s32[2,80]{1,0:T(2,128)S(1)}, s32[2,80]{1,0:T(2,128)}, u32[]{:S(2)}) copy-start(s32[2,80]{1,0:T(2,128)} %param.27) | copy-start | bytes 1924
  7.2 12.9 %copy-start.74 = (s32[2]{0:T(128)S(1)}, s32[2]{0:T(128)}, u32[]{:S(2)}) copy-start(s32[2]{0:T(128)} %param.28) | copy-start | bytes 28
  7.2 14.2 %copy-start.33 = (f32[205,384]{1,0:T(8,128)S(1)}, f32[205,384]{1,0:T(8,128)}, u32[]{:S(2)}) copy-start(f32[205,384]{1,0:T(8,128)} %param.32) | copy-start | bytes 944644
  7.2 124.7 %all-gather.5.cloned.1.call-start = ((), (), s32[]{:S(2)}) async-start(), calls=%async_computation.7 | async-start | bytes 15814656 | tf_op jit(solution)/shard_map/all_gather | solution.py:145
  8.2 29.5 %copy-start.69 = (s32[2,80]{1,0:T(2,128)S(1)}, s32[2,80]{1,0:T(2,128)}, u32[]{:S(2)}) copy-start(s32[2,80]{1,0:T(2,128)} %param.29) | copy-start | bytes 1924
  15.8 22.6 %all-to-all-start = ((bf16[8,2,1,197,48]{3,0,4,2,1:T(8,128)(2,1)}), bf16[8,2,1,197,48]{3,0,4,2,1:T(8,128)(2,1)S(1)}, u32[]{:S(2)}, u32[]{:S(2)}) async-start(bf16[8,2,1,197,48]{3,0,4,2,1:T(8,128)(2,1)} %copy.121), calls=%async_computation | async-start | bytes 786432 | tf_op jit(solution)/shard_map/all_to_all | solution.py:158
  21.4 131.8 %copy-start.72 = (pred[197]{0:T(512)(128)(4,1)}, pred[197]{0:T(512)(128)(4,1)S(1)}, u32[]{:S(2)}) copy-start(pred[197]{0:T(512)(128)(4,1)S(1)} %fusion.60) | copy-start | bytes 595
  37.6 94.3 %copy-start.38 = (f32[205,768]{1,0:T(8,128)}, f32[205,768]{1,0:T(8,128)S(1)}, u32[]{:S(2)}) copy-start(f32[205,768]{1,0:T(8,128)S(1)} %all_gather.18) | copy-start | bytes 1889284
  38.4 157.7 %copy-start.63 = (f32[768]{0:T(1024)}, f32[768]{0:T(1024)S(1)}, u32[]{:S(2)}) copy-start(f32[768]{0:T(1024)S(1)} %get-tuple-element.33) | copy-start | bytes 9220
  39.3 114.0 %all-to-all-start.1 = ((bf16[16,197,48]{1,2,0:T(8,128)(2,1)}), bf16[16,197,48]{1,2,0:T(8,128)(2,1)S(1)}, u32[]{:S(2)}, u32[]{:S(2)}) async-start(bf16[16,197,48]{1,2,0:T(8,128)(2,1)} %bitcast.12), calls=%async_computation.1 | async-start | bytes 786432 | tf_op jit(solution)/shard_map/all_to_all | solution.py:160
  45.4 190.8 %reduce-scatter.3.cloned.1.call-start = ((), (), s32[]{:S(2)}) async-start(), calls=%async_computation.4 | async-start | bytes 368640 | tf_op jit(solution)/shard_map/reduce_scatter | solution.py:226
  144.7 8.6 %copy-start.39 = (f32[205,768]{1,0:T(8,128)S(1)}, f32[205,768]{1,0:T(8,128)}, u32[]{:S(2)}) copy-start(f32[205,768]{1,0:T(8,128)} %copy-done.38) | copy-start | bytes 1889284
  155.3 100.5 %copy-start.3 = (f32[197,768]{1,0:T(8,128)}, f32[197,768]{1,0:T(8,128)S(1)}, u32[]{:S(2)}) copy-start(f32[197,768]{1,0:T(8,128)S(1)} %get-tuple-element.86) | copy-start | bytes 1815556
  164.2 16.8 %copy-start.57 = (f32[12,197]{1,0:T(8,128)}, f32[12,197]{1,0:T(8,128)S(1)}, u32[]{:S(2)}) copy-start(f32[12,197]{1,0:T(8,128)S(1)} %get-tuple-element.87) | copy-start | bytes 28372
  165.7 16.7 %copy-start.10 = (bf16[96,8,2,384]{3,1,2,0:T(8,128)(2,1)}, bf16[96,8,2,384]{3,1,2,0:T(8,128)(2,1)S(1)}, u32[]{:S(2)}) copy-start(bf16[96,8,2,384]{3,1,2,0:T(8,128)(2,1)S(1)} %copy.153) | copy-start | bytes 3538948
  182.4 10.6 %copy-start.31 = (bf16[12,64,197]{2,1,0:T(8,128)(2,1)}, bf16[12,64,197]{2,1,0:T(8,128)(2,1)S(1)}, u32[]{:S(2)}) copy-start(bf16[12,64,197]{2,1,0:T(8,128)(2,1)S(1)} %convolution_convert_fusion.7) | copy-start | bytes 907780
  182.9 24.5 %copy-start.5 = (f32[197,768]{1,0:T(8,128)}, f32[197,768]{1,0:T(8,128)S(1)}, u32[]{:S(2)}) copy-start(f32[197,768]{1,0:T(8,128)S(1)} %get-tuple-element.90) | copy-start | bytes 1815556
  183.0 63.2 %copy-start.61 = (f32[197]{0:T(256)}, f32[197]{0:T(256)S(1)}, u32[]{:S(2)}) copy-start(f32[197]{0:T(256)S(1)} %broadcast_multiply_fusion.7) | copy-start | bytes 2368
  183.2 63.0 %copy-start.67 = (f32[197]{0:T(256)}, f32[197]{0:T(256)S(1)}, u32[]{:S(2)}) copy-start(f32[197]{0:T(256)S(1)} %add_rsqrt_fusion.1) | copy-start | bytes 2368
  196.1 11.3 %copy-start.2 = (bf16[384,8,2,384]{3,1,2,0:T(8,128)(2,1)}, bf16[384,8,2,384]{3,1,2,0:T(8,128)(2,1)S(1)}, u32[]{:S(2)}) copy-start(bf16[384,8,2,384]{3,1,2,0:T(8,128)(2,1)S(1)} %copy.155) | copy-start | bytes 14155780
  196.2 19.5 %slice-start = ((s8[12582912]{0:T(1024)(128)(4,1)}), s8[4194304]{0:T(1024)(128)(4,1)S(1)}, s32[]{:S(2)}) async-start(s8[12582912]{0:T(1024)(128)(4,1)} %bitcast.225), calls=%async_computation.9 | async-start | bytes 8388608
  196.2 19.5 %slice-start.1 = ((s8[12582912]{0:T(1024)(128)(4,1)}), s8[4194304]{0:T(1024)(128)(4,1)S(1)}, s32[]{:S(2)}) async-start(s8[12582912]{0:T(1024)(128)(4,1)} %bitcast.225), calls=%async_computation.10 | async-start | bytes 8388608
  196.2 19.5 %slice-start.2 = ((s8[12582912]{0:T(1024)(128)(4,1)}), s8[4194304]{0:T(1024)(128)(4,1)S(1)}, s32[]{:S(2)}) async-start(s8[12582912]{0:T(1024)(128)(4,1)} %bitcast.225), calls=%async_computation.11 | async-start | bytes 8388608
  226.5 178.1 %all-reduce.7.cloned.1.call-start = ((), (), s32[]{:S(2)}) async-start(), calls=%async_computation.8 | async-start | bytes 13221888 | tf_op jit(solution)/shard_map/psum | solution.py:297
  231.2 8.2 %copy-start.76 = (f32[197,3072]{1,0:T(8,128)S(1)}, f32[197,3072]{1,0:T(8,128)}, u32[]{:S(2)}) copy-start(f32[197,3072]{1,0:T(8,128)} %get-tuple-element.77) | copy-start | bytes 7262212
  238.0 6.8 slice-start.3
  239.4 6.8 copy-start.24
  259.6 176.5 %all-reduce.5.cloned.1.call-start = ((), (), s32[]{:S(2)}) async-start(), calls=%async_computation.6 | async-start | bytes 638976 | tf_op jit(solution)/shard_map/psum | solution.py:297
  289.5 5.7 copy-start.26
  289.5 6.9 copy-start.8
  404.6 201.0 %reduce-scatter.5.cloned.1.call-start = ((), (), s32[]{:S(2)}) async-start(), calls=%async_computation.5 | async-start | bytes 15814656 | tf_op jit(solution)/shard_map/reduce_scatter | solution.py:294
  429.3 223.6 %copy-start.45 = (f32[48,384]{1,0:T(8,128)S(1)}, f32[48,384]{1,0:T(8,128)}, u32[]{:S(2)}) copy-start(f32[48,384]{1,0:T(8,128)} %param.31) | copy-start | bytes 221188
  429.3 223.6 %copy-start.53 = (f32[48,384]{1,0:T(8,128)S(1)}, f32[48,384]{1,0:T(8,128)}, u32[]{:S(2)}) copy-start(f32[48,384]{1,0:T(8,128)} %param.45) | copy-start | bytes 221188
  429.3 223.6 %copy-start.54 = (f32[48,384]{1,0:T(8,128)S(1)}, f32[48,384]{1,0:T(8,128)}, u32[]{:S(2)}) copy-start(f32[48,384]{1,0:T(8,128)} %param.38) | copy-start | bytes 221188
  436.0 217.6 %copy-start.37 = (f32[1,384,144]{1,2,0:T(8,128)S(1)}, f32[1,384,144]{1,2,0:T(8,128)}, u32[]{:S(2)}) copy-start(f32[1,384,144]{1,2,0:T(8,128)} %param.33) | copy-start | bytes 663556
  436.0 217.6 %copy-start.51 = (f32[1,384,144]{1,2,0:T(8,128)S(1)}, f32[1,384,144]{1,2,0:T(8,128)}, u32[]{:S(2)}) copy-start(f32[1,384,144]{1,2,0:T(8,128)} %param.47) | copy-start | bytes 663556
  436.0 217.6 %copy-start.52 = (f32[1,384,144]{1,2,0:T(8,128)S(1)}, f32[1,384,144]{1,2,0:T(8,128)}, u32[]{:S(2)}) copy-start(f32[1,384,144]{1,2,0:T(8,128)} %param.40) | copy-start | bytes 663556
  436.0 218.6 %copy-start.46 = (f32[1,48,384]{2,1,0:T(8,128)S(1)}, f32[1,48,384]{2,1,0:T(8,128)}, u32[]{:S(2)}) copy-start(f32[1,48,384]{2,1,0:T(8,128)} %param.34) | copy-start | bytes 221188
  436.0 218.6 %copy-start.55 = (f32[1,48,384]{2,1,0:T(8,128)S(1)}, f32[1,48,384]{2,1,0:T(8,128)}, u32[]{:S(2)}) copy-start(f32[1,48,384]{2,1,0:T(8,128)} %param.48) | copy-start | bytes 221188
  436.0 218.6 %copy-start.56 = (f32[1,48,384]{2,1,0:T(8,128)S(1)}, f32[1,48,384]{2,1,0:T(8,128)}, u32[]{:S(2)}) copy-start(f32[1,48,384]{2,1,0:T(8,128)} %param.41) | copy-start | bytes 221188
  436.0 219.3 %copy-start.35 = (f32[1,384,192]{1,2,0:T(8,128)S(1)}, f32[1,384,192]{1,2,0:T(8,128)}, u32[]{:S(2)}) copy-start(f32[1,384,192]{1,2,0:T(8,128)} %param.35) | copy-start | bytes 884740
  436.0 219.3 %copy-start.47 = (f32[1,384,192]{1,2,0:T(8,128)S(1)}, f32[1,384,192]{1,2,0:T(8,128)}, u32[]{:S(2)}) copy-start(f32[1,384,192]{1,2,0:T(8,128)} %param.49) | copy-start | bytes 884740
  436.0 219.2 %copy-start.48 = (f32[1,384,192]{1,2,0:T(8,128)S(1)}, f32[1,384,192]{1,2,0:T(8,128)}, u32[]{:S(2)}) copy-start(f32[1,384,192]{1,2,0:T(8,128)} %param.42) | copy-start | bytes 884740
  657.4 29.7 %copy-start.34 = (f32[205,384]{1,0:T(8,128)S(1)}, f32[205,384]{1,0:T(8,128)}, u32[]{:S(2)}) copy-start(f32[205,384]{1,0:T(8,128)} %param.32) | copy-start | bytes 944644
  657.4 29.7 %copy-start.42 = (bf16[205,768]{1,0:T(8,128)(2,1)S(1)}, bf16[205,768]{1,0:T(8,128)(2,1)}, u32[]{:S(2)}) copy-start(bf16[205,768]{1,0:T(8,128)(2,1)} %all-reduce.5.cloned.1.call-done) | copy-start | bytes 944644
  657.4 29.7 %copy-start.43 = (f32[205,384]{1,0:T(8,128)S(1)}, f32[205,384]{1,0:T(8,128)}, u32[]{:S(2)}) copy-start(f32[205,384]{1,0:T(8,128)} %param.46) | copy-start | bytes 944644
  657.4 29.7 %copy-start.44 = (f32[205,384]{1,0:T(8,128)S(1)}, f32[205,384]{1,0:T(8,128)}, u32[]{:S(2)}) copy-start(f32[205,384]{1,0:T(8,128)} %param.39) | copy-start | bytes 944644
  657.4 30.8 %copy-start.1 = (s32[2,80]{1,0:T(2,128)S(1)}, s32[2,80]{1,0:T(2,128)}, u32[]{:S(2)}) copy-start(s32[2,80]{1,0:T(2,128)} %param.27) | copy-start | bytes 1924
  (41 other events, 97.0 us)
Sparse Core Ops, SparseCore 0:
  13.0 118.8 all-gather.4
  226.6 9.6 reduce-scatter.2
  259.7 144.8 all-reduce.6
  406.8 23.8 all-reduce.4
  436.7 168.8 reduce-scatter.4
